TPU v7x, 256 devices: a whole 4x4x8 slice. The times are simulated.
256 devices in a mesh: span: 8 (over x_lo, y), wide: 32 (over x_hi, z, core).
Axes of the slice: x: 4 (x_hi: 2, x_lo: 2; x = x_hi * 2 + x_lo), y: 4, z: 8, core: 2. Of those that a mesh axis runs over, the one named last changes fastest.
Arguments:
- queries: bfloat16 [36864, 4096], P(('span', 'wide')), may hold values from -28 to 28
- keys: bfloat16 [36864, 4096], P(('span', 'wide')), may hold values from -9.6 to 9.6
- values: bfloat16 [36864, 4096], P(('span', 'wide')), may hold values from -12 to 12
- windows: int32 [96, 12], replicated, may hold values from -1 to 95, as said below
Outputs:
- attended: bfloat16 [36864, 4096], P(('span', 'wide'))
Inputs may be any that keep to these rules, and one draw needn't show every extreme that they name: `windows`: row i lists the tiles that tile i attends to, where a tile's time tile is its index // 6: every listed tile lies at most one time tile from tile i's, the entries of a row are distinct, tile i is in row i, and -1 marks an empty slot.
All inputs are finite; a program needn't handle non-finite values.
Results may differ from a plain program's by a relative error of at most 0.0031.
Values may be sent and summed in bfloat16 or wider, within the bound.
A program may use at most 128 MiB of HBM per device.

v0:
```python
import jax
import jax.numpy as jnp
from jax import lax
from jax.sharding import PartitionSpec as P

HD = 128
TILE = 384
HT = 2
WT = 3
NBR = 12


NEG_FILL = -1e30


def extended_2(cells, sides, width):
    for axis, dim in sides:
        count = lax.axis_size(axis)
        ends = count - 1
        head = lax.slice_in_dim(cells, 0, width, axis=dim)
        tail = lax.slice_in_dim(cells, cells.shape[dim] - width, cells.shape[dim], axis=dim)
        cells = jnp.concatenate(
            [
                lax.ppermute(tail, axis, [(i, (i + 1) % count) for i in range(ends)]),
                cells,
                lax.ppermute(head, axis, [((i + 1) % count, i) for i in range(ends)]),
            ],
            axis=dim,
        )
    return cells


def extend(local_keys, local_values):
    plane = HT * WT
    paired = jnp.stack((local_keys, local_values), axis=0)
    time_local = paired.shape[1] // (plane * TILE)
    paired = paired.reshape(2, time_local, plane * TILE, paired.shape[2], paired.shape[3])
    return extended_2(paired, (("span", 1),), 1)


def weigh(scores, allowed):
    masked = jnp.where(allowed, scores, NEG_FILL)
    highest = jnp.max(masked, axis=(3, 4), keepdims=True)
    expo = jnp.exp(masked - highest)
    summed = jnp.sum(expo, axis=(3, 4))
    return (expo.astype(jnp.bfloat16), jnp.moveaxis(summed, 1, 2))


def body(queries, keys, values, windows):
    span_index = lax.axis_index("span")
    row_count = queries.shape[0]
    heads_total = queries.shape[1] // HD
    shaped_q = queries.reshape(row_count, heads_total, HD)
    shaped_k = keys.reshape(row_count, heads_total, HD)
    shaped_v = values.reshape(row_count, heads_total, HD)
    local_q, local_k, local_v = (
        lax.all_to_all(shaped_q, "wide", split_axis=1, concat_axis=0, tiled=True),
        lax.all_to_all(shaped_k, "wide", split_axis=1, concat_axis=0, tiled=True),
        lax.all_to_all(shaped_v, "wide", split_axis=1, concat_axis=0, tiled=True),
    )
    extended = extend(local_k, local_v)
    span_tokens = local_q.shape[0]
    head_local = local_q.shape[1]
    plane = HT * WT
    tile_count = span_tokens // TILE
    time_local = tile_count // plane
    local_tiles = (time_local + 2) * plane
    key_tiles = extended[0].reshape(local_tiles, TILE, head_local, HD)
    value_tiles = extended[1].reshape(local_tiles, TILE, head_local, HD)
    score_scale = HD ** (-0.5)
    first_tile = span_index * tile_count
    own_windows = lax.dynamic_slice_in_dim(windows, first_tile, tile_count, 0)
    listed_ok = own_windows >= 0
    local_ids = jnp.where(listed_ok, own_windows - first_tile + plane, 0)
    group_count = tile_count // 2
    query_groups = local_q.reshape(group_count, 2, TILE, head_local, HD)
    id_groups = local_ids.reshape(group_count, 2, NBR)
    ok_groups = listed_ok.reshape(group_count, 2, NBR)

    def attend(item):
        query_block, id_block, ok_block = item
        key_block = key_tiles[id_block]
        value_block = value_tiles[id_block]
        scores = (
            jnp.einsum(
                "gqhd,gnthd->ghqnt", query_block, key_block, preferred_element_type=jnp.float32
            )
            * score_scale
        )
        weights, summed = weigh(scores, ok_block[:, None, None, :, None])
        mixed = jnp.einsum(
            "ghqnt,gnthd->gqhd", weights, value_block, preferred_element_type=jnp.float32
        )
        return (mixed / summed[:, :, :, None]).astype(jnp.bfloat16)

    attended = lax.map(attend, (query_groups, id_groups, ok_groups))
    attended = attended.reshape(span_tokens, head_local, HD)
    returned = lax.all_to_all(attended, "wide", split_axis=0, concat_axis=1, tiled=True)
    return returned.reshape(returned.shape[0], returned.shape[1] * HD)


def solution(mesh):
    return jax.shard_map(
        body,
        mesh=mesh,
        in_specs=(
            P(("span", "wide"), None),
            P(("span", "wide"), None),
            P(("span", "wide"), None),
            P(),
        ),
        out_specs=P(("span", "wide"), None),
        check_vma=False,
    )
```

profile of v0, /device:TPU:1, one launch (start us, length us, event | category | flops | bytes accessed | tf_op | source)
XLA Modules:
  0.0 392.7 jit_solution(13244441713853635634)
XLA Ops:
  2.5 12.6 %all-to-all-start = ((bf16[144,32,128]{2,0,1:T(8,128)(2,1)}), bf16[144,32,128]{2,0,1:T(8,128)(2,1)S(1)}, u32[]{:S(2)}, u32[]{:S(2)}) async-start(bf16[144,32,128]{2,0,1:T(8,128)(2,1)} %copy_bitcast_fusion.3), calls=%async_computation | async-start | bytes 2359296 | tf_op jit(solution)/shard_map/all_to_all | solution.py:58
  16.3 29.3 %all-to-all-done = bf16[144,32,128]{2,0,1:T(8,128)(2,1)S(1)} async-done(((bf16[144,32,128]{2,0,1:T(8,128)(2,1)}), bf16[144,32,128]{2,0,1:T(8,128)(2,1)S(1)}, u32[]{:S(2)}, u32[]{:S(2)}) %all-to-all-start) | async-done | bytes 1179680 | tf_op jit(solution)/shard_map/all_to_all | solution.py:58
  45.6 39.3 %all_to_all.60 = bf16[144,32,128]{2,0,1:T(8,128)(2,1)S(1)} all-to-all(bf16[144,32,128]{2,0,1:T(8,128)(2,1)} %copy_bitcast_fusion.2), channel_id=1, replica_groups=mesh['span'=8,'wide'=32] {'wide'}, dimensions={1} | all-to-all | bytes 2359296 | tf_op jit(solution)/shard_map/all_to_all | solution.py:59
  86.5 4.2 %collective-permute-start = (bf16[2,1,2304,1,128]{4,2,1,3,0:T(8,128)(2,1)}, bf16[2,1,2304,1,128]{4,2,1,3,0:T(8,128)(2,1)}, u32[]{:S(2)}, u32[]{:S(2)}) collective-permute-start(bf16[2,1,2304,1,128]{4,2,1,3,0:T(8,128)(2,1)} %get-tuple-element.63), channel_id=1, source_target_pairs={{0,32},{32,64},{64,96},{96,128},{128,160},{160,192},{192,224},{1,3... | collective-permute-start | bytes 3538952 | tf_op jit(solution)/shard_map/ppermute | solution.py:24
  93.4 6.1 %all-to-all-start.2 = ((bf16[144,32,128]{2,0,1:T(8,128)(2,1)}), bf16[144,32,128]{2,0,1:T(8,128)(2,1)}, u32[]{:S(2)}, u32[]{:S(2)}) async-start(bf16[144,32,128]{2,0,1:T(8,128)(2,1)} %copy_bitcast_fusion.1), calls=%async_computation.2 | async-start | bytes 2359296 | tf_op jit(solution)/shard_map/all_to_all | solution.py:57
  102.3 11.4 %collective-permute-done = bf16[2,1,2304,1,128]{4,2,1,3,0:T(8,128)(2,1)} collective-permute-done((bf16[2,1,2304,1,128]{4,2,1,3,0:T(8,128)(2,1)}, bf16[2,1,2304,1,128]{4,2,1,3,0:T(8,128)(2,1)}, u32[]{:S(2)}, u32[]{:S(2)}) %collective-permute-start) | collective-permute-done | bytes 1179680 | tf_op jit(solution)/shard_map/ppermute | solution.py:24
  113.7 5.0 %collective-permute-done.1 = bf16[2,1,2304,1,128]{4,2,1,3,0:T(8,128)(2,1)} collective-permute-done((bf16[2,1,2304,1,128]{4,2,1,3,0:T(8,128)(2,1)}, bf16[2,1,2304,1,128]{4,2,1,3,0:T(8,128)(2,1)}, u32[]{:S(2)}, u32[]{:S(2)}) %collective-permute-start.1) | collective-permute-done | bytes 1179680 | tf_op jit(solution)/shard_map/ppermute | solution.py:26
  122.4 8.0 %all-to-all-done.2 = bf16[144,32,128]{2,0,1:T(8,128)(2,1)} async-done(((bf16[144,32,128]{2,0,1:T(8,128)(2,1)}), bf16[144,32,128]{2,0,1:T(8,128)(2,1)}, u32[]{:S(2)}, u32[]{:S(2)}) %all-to-all-start.2) | async-done | bytes 1179680 | tf_op jit(solution)/shard_map/all_to_all | solution.py:57
  130.3 213.3 %while.10 = (s32[]{:T(128)}, bf16[6,2,384,1,128]{4,2,1,0,3:T(8,128)(2,1)}, s32[6,2,12]{2,1,0:T(2,128)}, bf16[24,384,1,128]{3,1,0,2:T(8,128)(2,1)}, pred[6,2,12]{...) while((s32[]{:T(128)}, ...), condition=%wide.region_3.4_spmd, body=%wide.region_0.3_spmd.sunk | while | flops 1851063808 | bytes 86135744 | solution.py:96
  135.1 7.0 %fusion.40 = (f32[2,384]{1,0:T(2,128)S(1)}, f32[2,384,12,384]{1,3,2,0:T(8,128)}) fusion(pred[2,12]{1,0:T(4,128)(4,1)S(1)} %dynamic-slice_bitcast_fusion.2, bf16[2,12,384,128]{3,2,1,0:T(8,128)(2,1)S(1)} %bitcast.99, bf16[6,2,384,1,128]{4,2,1,3,0:T(8,128)(2,1)} %get-tuple-element.133, s32[]{:T(128)} %get-tuple-element.120), kind=kOutput, calls=%fused_computation.4.clone.1 | convolution fusion | flops 916585728 | bytes 16715288 | tf_op jit(solution)/shard_map/while/body/eval_jaxpr/gqhd,gnthd->ghqnt/dot_general | solution.py:85
  142.1 8.2 %fusion.41 = f32[2,384]{1,0:T(2,128)S(1)} fusion(f32[2,384,12,384]{1,3,2,0:T(8,128)} %get-tuple-element.110, f32[2,384]{1,0:T(2,128)S(1)} %get-tuple-element.111, pred[2,12]{1,0:T(4,128)(4,1)S(1)} %dynamic-slice_bitcast_fusion.2), kind=kLoop, calls=%fused_computation.5.clone.1 | loop fusion | flops 14155008 | bytes 14161944 | tf_op jit(solution)/shard_map/while/body/eval_jaxpr/reduce_sum | solution.py:45
  152.6 9.9 %fusion.42 = bf16[1,2,384,1,128]{2,4,1,3,0:T(8,128)(2,1)} fusion(bf16[2,12,384,128]{3,2,1,0:T(8,128)(2,1)} %bitcast.104, f32[2,384,12,384]{1,3,2,0:T(8,128)} %get-tuple-element.110, f32[2,384]{1,0:T(2,128)S(1)} %get-tuple-element.111, pred[2,12]{1,0:T(4,128)(4,1)S(1)} %dynamic-slice_bitcast_fusion.2, f32[2,384]{1,0:T(2,128)S(1)} %fusion.41), kind=kOutput, calls=%fused_computation.12.clone.1 | convolution fusion | flops 920322048 | bytes 16717848 | tf_op jit(solution)/shard_map/while/body/eval_jaxpr/ghqnt,gnthd->gqhd/dot_general | solution.py:91
  167.3 2.7 gather_fusion.1
  170.7 7.0 %fusion.40 = (f32[2,384]{1,0:T(2,128)S(1)}, f32[2,384,12,384]{1,3,2,0:T(8,128)}) fusion(pred[2,12]{1,0:T(4,128)(4,1)S(1)} %dynamic-slice_bitcast_fusion.2, bf16[2,12,384,128]{3,2,1,0:T(8,128)(2,1)S(1)} %bitcast.99, bf16[6,2,384,1,128]{4,2,1,3,0:T(8,128)(2,1)} %get-tuple-element.133, s32[]{:T(128)} %get-tuple-element.120), kind=kOutput, calls=%fused_computation.4.clone.1 | convolution fusion | flops 916585728 | bytes 16715288 | tf_op jit(solution)/shard_map/while/body/eval_jaxpr/gqhd,gnthd->ghqnt/dot_general | solution.py:85
  177.7 8.2 %fusion.41 = f32[2,384]{1,0:T(2,128)S(1)} fusion(f32[2,384,12,384]{1,3,2,0:T(8,128)} %get-tuple-element.110, f32[2,384]{1,0:T(2,128)S(1)} %get-tuple-element.111, pred[2,12]{1,0:T(4,128)(4,1)S(1)} %dynamic-slice_bitcast_fusion.2), kind=kLoop, calls=%fused_computation.5.clone.1 | loop fusion | flops 14155008 | bytes 14161944 | tf_op jit(solution)/shard_map/while/body/eval_jaxpr/reduce_sum | solution.py:45
  188.2 9.9 %fusion.42 = bf16[1,2,384,1,128]{2,4,1,3,0:T(8,128)(2,1)} fusion(bf16[2,12,384,128]{3,2,1,0:T(8,128)(2,1)} %bitcast.104, f32[2,384,12,384]{1,3,2,0:T(8,128)} %get-tuple-element.110, f32[2,384]{1,0:T(2,128)S(1)} %get-tuple-element.111, pred[2,12]{1,0:T(4,128)(4,1)S(1)} %dynamic-slice_bitcast_fusion.2, f32[2,384]{1,0:T(2,128)S(1)} %fusion.41), kind=kOutput, calls=%fused_computation.12.clone.1 | convolution fusion | flops 920322048 | bytes 16717848 | tf_op jit(solution)/shard_map/while/body/eval_jaxpr/ghqnt,gnthd->gqhd/dot_general | solution.py:91
  206.2 7.0 %fusion.40 = (f32[2,384]{1,0:T(2,128)S(1)}, f32[2,384,12,384]{1,3,2,0:T(8,128)}) fusion(pred[2,12]{1,0:T(4,128)(4,1)S(1)} %dynamic-slice_bitcast_fusion.2, bf16[2,12,384,128]{3,2,1,0:T(8,128)(2,1)S(1)} %bitcast.99, bf16[6,2,384,1,128]{4,2,1,3,0:T(8,128)(2,1)} %get-tuple-element.133, s32[]{:T(128)} %get-tuple-element.120), kind=kOutput, calls=%fused_computation.4.clone.1 | convolution fusion | flops 916585728 | bytes 16715288 | tf_op jit(solution)/shard_map/while/body/eval_jaxpr/gqhd,gnthd->ghqnt/dot_general | solution.py:85
  213.3 8.2 %fusion.41 = f32[2,384]{1,0:T(2,128)S(1)} fusion(f32[2,384,12,384]{1,3,2,0:T(8,128)} %get-tuple-element.110, f32[2,384]{1,0:T(2,128)S(1)} %get-tuple-element.111, pred[2,12]{1,0:T(4,128)(4,1)S(1)} %dynamic-slice_bitcast_fusion.2), kind=kLoop, calls=%fused_computation.5.clone.1 | loop fusion | flops 14155008 | bytes 14161944 | tf_op jit(solution)/shard_map/while/body/eval_jaxpr/reduce_sum | solution.py:45
  223.8 9.9 %fusion.42 = bf16[1,2,384,1,128]{2,4,1,3,0:T(8,128)(2,1)} fusion(bf16[2,12,384,128]{3,2,1,0:T(8,128)(2,1)} %bitcast.104, f32[2,384,12,384]{1,3,2,0:T(8,128)} %get-tuple-element.110, f32[2,384]{1,0:T(2,128)S(1)} %get-tuple-element.111, pred[2,12]{1,0:T(4,128)(4,1)S(1)} %dynamic-slice_bitcast_fusion.2, f32[2,384]{1,0:T(2,128)S(1)} %fusion.41), kind=kOutput, calls=%fused_computation.12.clone.1 | convolution fusion | flops 920322048 | bytes 16717848 | tf_op jit(solution)/shard_map/while/body/eval_jaxpr/ghqnt,gnthd->gqhd/dot_general | solution.py:91
  238.4 2.7 gather_fusion.1
  241.7 7.0 %fusion.40 = (f32[2,384]{1,0:T(2,128)S(1)}, f32[2,384,12,384]{1,3,2,0:T(8,128)}) fusion(pred[2,12]{1,0:T(4,128)(4,1)S(1)} %dynamic-slice_bitcast_fusion.2, bf16[2,12,384,128]{3,2,1,0:T(8,128)(2,1)S(1)} %bitcast.99, bf16[6,2,384,1,128]{4,2,1,3,0:T(8,128)(2,1)} %get-tuple-element.133, s32[]{:T(128)} %get-tuple-element.120), kind=kOutput, calls=%fused_computation.4.clone.1 | convolution fusion | flops 916585728 | bytes 16715288 | tf_op jit(solution)/shard_map/while/body/eval_jaxpr/gqhd,gnthd->ghqnt/dot_general | solution.py:85
  248.8 8.2 %fusion.41 = f32[2,384]{1,0:T(2,128)S(1)} fusion(f32[2,384,12,384]{1,3,2,0:T(8,128)} %get-tuple-element.110, f32[2,384]{1,0:T(2,128)S(1)} %get-tuple-element.111, pred[2,12]{1,0:T(4,128)(4,1)S(1)} %dynamic-slice_bitcast_fusion.2), kind=kLoop, calls=%fused_computation.5.clone.1 | loop fusion | flops 14155008 | bytes 14161944 | tf_op jit(solution)/shard_map/while/body/eval_jaxpr/reduce_sum | solution.py:45
  259.3 9.9 %fusion.42 = bf16[1,2,384,1,128]{2,4,1,3,0:T(8,128)(2,1)} fusion(bf16[2,12,384,128]{3,2,1,0:T(8,128)(2,1)} %bitcast.104, f32[2,384,12,384]{1,3,2,0:T(8,128)} %get-tuple-element.110, f32[2,384]{1,0:T(2,128)S(1)} %get-tuple-element.111, pred[2,12]{1,0:T(4,128)(4,1)S(1)} %dynamic-slice_bitcast_fusion.2, f32[2,384]{1,0:T(2,128)S(1)} %fusion.41), kind=kOutput, calls=%fused_computation.12.clone.1 | convolution fusion | flops 920322048 | bytes 16717848 | tf_op jit(solution)/shard_map/while/body/eval_jaxpr/ghqnt,gnthd->gqhd/dot_general | solution.py:91
  277.3 7.0 %fusion.40 = (f32[2,384]{1,0:T(2,128)S(1)}, f32[2,384,12,384]{1,3,2,0:T(8,128)}) fusion(pred[2,12]{1,0:T(4,128)(4,1)S(1)} %dynamic-slice_bitcast_fusion.2, bf16[2,12,384,128]{3,2,1,0:T(8,128)(2,1)S(1)} %bitcast.99, bf16[6,2,384,1,128]{4,2,1,3,0:T(8,128)(2,1)} %get-tuple-element.133, s32[]{:T(128)} %get-tuple-element.120), kind=kOutput, calls=%fused_computation.4.clone.1 | convolution fusion | flops 916585728 | bytes 16715288 | tf_op jit(solution)/shard_map/while/body/eval_jaxpr/gqhd,gnthd->ghqnt/dot_general | solution.py:85
  284.4 8.2 %fusion.41 = f32[2,384]{1,0:T(2,128)S(1)} fusion(f32[2,384,12,384]{1,3,2,0:T(8,128)} %get-tuple-element.110, f32[2,384]{1,0:T(2,128)S(1)} %get-tuple-element.111, pred[2,12]{1,0:T(4,128)(4,1)S(1)} %dynamic-slice_bitcast_fusion.2), kind=kLoop, calls=%fused_computation.5.clone.1 | loop fusion | flops 14155008 | bytes 14161944 | tf_op jit(solution)/shard_map/while/body/eval_jaxpr/reduce_sum | solution.py:45
  294.9 9.9 %fusion.42 = bf16[1,2,384,1,128]{2,4,1,3,0:T(8,128)(2,1)} fusion(bf16[2,12,384,128]{3,2,1,0:T(8,128)(2,1)} %bitcast.104, f32[2,384,12,384]{1,3,2,0:T(8,128)} %get-tuple-element.110, f32[2,384]{1,0:T(2,128)S(1)} %get-tuple-element.111, pred[2,12]{1,0:T(4,128)(4,1)S(1)} %dynamic-slice_bitcast_fusion.2, f32[2,384]{1,0:T(2,128)S(1)} %fusion.41), kind=kOutput, calls=%fused_computation.12.clone.1 | convolution fusion | flops 920322048 | bytes 16717848 | tf_op jit(solution)/shard_map/while/body/eval_jaxpr/ghqnt,gnthd->gqhd/dot_general | solution.py:91
  312.9 7.0 %fusion.40 = (f32[2,384]{1,0:T(2,128)S(1)}, f32[2,384,12,384]{1,3,2,0:T(8,128)}) fusion(pred[2,12]{1,0:T(4,128)(4,1)S(1)} %dynamic-slice_bitcast_fusion.2, bf16[2,12,384,128]{3,2,1,0:T(8,128)(2,1)S(1)} %bitcast.99, bf16[6,2,384,1,128]{4,2,1,3,0:T(8,128)(2,1)} %get-tuple-element.133, s32[]{:T(128)} %get-tuple-element.120), kind=kOutput, calls=%fused_computation.4.clone.1 | convolution fusion | flops 916585728 | bytes 16715288 | tf_op jit(solution)/shard_map/while/body/eval_jaxpr/gqhd,gnthd->ghqnt/dot_general | solution.py:85
  319.9 8.2 %fusion.41 = f32[2,384]{1,0:T(2,128)S(1)} fusion(f32[2,384,12,384]{1,3,2,0:T(8,128)} %get-tuple-element.110, f32[2,384]{1,0:T(2,128)S(1)} %get-tuple-element.111, pred[2,12]{1,0:T(4,128)(4,1)S(1)} %dynamic-slice_bitcast_fusion.2), kind=kLoop, calls=%fused_computation.5.clone.1 | loop fusion | flops 14155008 | bytes 14161944 | tf_op jit(solution)/shard_map/while/body/eval_jaxpr/reduce_sum | solution.py:45
  330.4 9.9 %fusion.42 = bf16[1,2,384,1,128]{2,4,1,3,0:T(8,128)(2,1)} fusion(bf16[2,12,384,128]{3,2,1,0:T(8,128)(2,1)} %bitcast.104, f32[2,384,12,384]{1,3,2,0:T(8,128)} %get-tuple-element.110, f32[2,384]{1,0:T(2,128)S(1)} %get-tuple-element.111, pred[2,12]{1,0:T(4,128)(4,1)S(1)} %dynamic-slice_bitcast_fusion.2, f32[2,384]{1,0:T(2,128)S(1)} %fusion.41), kind=kOutput, calls=%fused_computation.12.clone.1 | convolution fusion | flops 920322048 | bytes 16717848 | tf_op jit(solution)/shard_map/while/body/eval_jaxpr/ghqnt,gnthd->gqhd/dot_general | solution.py:91
  344.2 2.8 reduce.4
  347.3 39.1 %all_to_all.61 = bf16[32,2,9216]{2,1,0:T(2,128)(2,1)} all-to-all(bf16[32,2,9216]{2,1,0:T(2,128)(2,1)S(1)} %reshape.130), channel_id=1, replica_groups=mesh['span'=8,'wide'=32] {'wide'}, dimensions={0} | all-to-all | bytes 2359296 | tf_op jit(solution)/shard_map/all_to_all | solution.py:98
  386.5 4.3 %reshape.131 = bf16[4608,1,128]{2,1,0:T(2,128)(2,1)S(1)} reshape(bf16[32,2,9216]{2,1,0:T(2,128)(2,1)} %all_to_all.61) | data formatting | bytes 2359296
  (108 shorter events, 74.3 us)
Async XLA Ops:
  0.0 1.3 copy-start
  0.0 15.1 %copy-start.4 = (bf16[144,4096]{1,0:T(8,128)(2,1)S(1)}, bf16[144,4096]{1,0:T(8,128)(2,1)}, u32[]{:S(2)}) copy-start(bf16[144,4096]{1,0:T(8,128)(2,1)} %param.8) | copy-start | bytes 3538948
  2.5 43.2 %all-to-all-start = ((bf16[144,32,128]{2,0,1:T(8,128)(2,1)}), bf16[144,32,128]{2,0,1:T(8,128)(2,1)S(1)}, u32[]{:S(2)}, u32[]{:S(2)}) async-start(bf16[144,32,128]{2,0,1:T(8,128)(2,1)} %copy_bitcast_fusion.3), calls=%async_computation | async-start | bytes 2359296 | tf_op jit(solution)/shard_map/all_to_all | solution.py:58
  84.9 7.3 %copy-start.5 = (bf16[144,4096]{1,0:T(8,128)(2,1)S(1)}, bf16[144,4096]{1,0:T(8,128)(2,1)}, u32[]{:S(2)}) copy-start(bf16[144,4096]{1,0:T(8,128)(2,1)} %param.6) | copy-start | bytes 3538948
  86.5 27.2 %collective-permute-start = (bf16[2,1,2304,1,128]{4,2,1,3,0:T(8,128)(2,1)}, bf16[2,1,2304,1,128]{4,2,1,3,0:T(8,128)(2,1)}, u32[]{:S(2)}, u32[]{:S(2)}) collective-permute-start(bf16[2,1,2304,1,128]{4,2,1,3,0:T(8,128)(2,1)} %get-tuple-element.63), channel_id=1, source_target_pairs={{0,32},{32,64},{64,96},{96,128},{128,160},{160,192},{192,224},{1,3... | collective-permute-start | bytes 3538952 | tf_op jit(solution)/shard_map/ppermute | solution.py:24
  90.8 8.8 %copy-start.6 = (s32[96,12]{0,1:T(8,128)S(1)}, s32[96,12]{0,1:T(8,128)}, u32[]{:S(2)}) copy-start(s32[96,12]{0,1:T(8,128)} %param.9) | copy-start | bytes 13828
  90.8 27.9 %collective-permute-start.1 = (bf16[2,1,2304,1,128]{4,2,1,3,0:T(8,128)(2,1)}, bf16[2,1,2304,1,128]{4,2,1,3,0:T(8,128)(2,1)}, u32[]{:S(2)}, u32[]{:S(2)}) collective-permute-start(bf16[2,1,2304,1,128]{4,2,1,3,0:T(8,128)(2,1)} %get-tuple-element.64), channel_id=1, source_target_pairs={{32,0},{64,32},{96,64},{128,96},{160,128},{192,160},{224,192},{33,... | collective-permute-start | bytes 3538952 | tf_op jit(solution)/shard_map/ppermute | solution.py:26
  93.4 36.9 %all-to-all-start.2 = ((bf16[144,32,128]{2,0,1:T(8,128)(2,1)}), bf16[144,32,128]{2,0,1:T(8,128)(2,1)}, u32[]{:S(2)}, u32[]{:S(2)}) async-start(bf16[144,32,128]{2,0,1:T(8,128)(2,1)} %copy_bitcast_fusion.1), calls=%async_computation.2 | async-start | bytes 2359296 | tf_op jit(solution)/shard_map/all_to_all | solution.py:57
  130.3 1.4 copy-start.1
  142.1 8.2 %copy-start.3 = (bf16[24,384,1,128]{3,1,0,2:T(8,128)(2,1)S(1)}, bf16[24,384,1,128]{3,1,0,2:T(8,128)(2,1)}, u32[]{:S(2)}) copy-start(bf16[24,384,1,128]{3,1,0,2:T(8,128)(2,1)} %get-tuple-element.131) | copy-start | bytes 7077892 | tf_op jit(solution)/shard_map/while
  152.6 13.2 %copy-start.2 = (bf16[24,384,1,128]{3,1,0,2:T(8,128)(2,1)S(1)}, bf16[24,384,1,128]{3,1,0,2:T(8,128)(2,1)}, u32[]{:S(2)}) copy-start(bf16[24,384,1,128]{3,1,0,2:T(8,128)(2,1)} %copy-done.1) | copy-start | bytes 7077892 | tf_op jit(solution)/shard_map/while
  165.9 1.4 copy-start.1
  177.7 8.2 %copy-start.3 = (bf16[24,384,1,128]{3,1,0,2:T(8,128)(2,1)S(1)}, bf16[24,384,1,128]{3,1,0,2:T(8,128)(2,1)}, u32[]{:S(2)}) copy-start(bf16[24,384,1,128]{3,1,0,2:T(8,128)(2,1)} %get-tuple-element.131) | copy-start | bytes 7077892 | tf_op jit(solution)/shard_map/while
  188.2 13.2 %copy-start.2 = (bf16[24,384,1,128]{3,1,0,2:T(8,128)(2,1)S(1)}, bf16[24,384,1,128]{3,1,0,2:T(8,128)(2,1)}, u32[]{:S(2)}) copy-start(bf16[24,384,1,128]{3,1,0,2:T(8,128)(2,1)} %copy-done.1) | copy-start | bytes 7077892 | tf_op jit(solution)/shard_map/while
  201.5 1.4 copy-start.1
  213.2 8.2 %copy-start.3 = (bf16[24,384,1,128]{3,1,0,2:T(8,128)(2,1)S(1)}, bf16[24,384,1,128]{3,1,0,2:T(8,128)(2,1)}, u32[]{:S(2)}) copy-start(bf16[24,384,1,128]{3,1,0,2:T(8,128)(2,1)} %get-tuple-element.131) | copy-start | bytes 7077892 | tf_op jit(solution)/shard_map/while
  223.8 13.2 %copy-start.2 = (bf16[24,384,1,128]{3,1,0,2:T(8,128)(2,1)S(1)}, bf16[24,384,1,128]{3,1,0,2:T(8,128)(2,1)}, u32[]{:S(2)}) copy-start(bf16[24,384,1,128]{3,1,0,2:T(8,128)(2,1)} %copy-done.1) | copy-start | bytes 7077892 | tf_op jit(solution)/shard_map/while
  237.0 1.4 copy-start.1
  248.8 8.2 %copy-start.3 = (bf16[24,384,1,128]{3,1,0,2:T(8,128)(2,1)S(1)}, bf16[24,384,1,128]{3,1,0,2:T(8,128)(2,1)}, u32[]{:S(2)}) copy-start(bf16[24,384,1,128]{3,1,0,2:T(8,128)(2,1)} %get-tuple-element.131) | copy-start | bytes 7077892 | tf_op jit(solution)/shard_map/while
  259.3 13.2 %copy-start.2 = (bf16[24,384,1,128]{3,1,0,2:T(8,128)(2,1)S(1)}, bf16[24,384,1,128]{3,1,0,2:T(8,128)(2,1)}, u32[]{:S(2)}) copy-start(bf16[24,384,1,128]{3,1,0,2:T(8,128)(2,1)} %copy-done.1) | copy-start | bytes 7077892 | tf_op jit(solution)/shard_map/while
  272.6 1.4 copy-start.1
  284.4 8.2 %copy-start.3 = (bf16[24,384,1,128]{3,1,0,2:T(8,128)(2,1)S(1)}, bf16[24,384,1,128]{3,1,0,2:T(8,128)(2,1)}, u32[]{:S(2)}) copy-start(bf16[24,384,1,128]{3,1,0,2:T(8,128)(2,1)} %get-tuple-element.131) | copy-start | bytes 7077892 | tf_op jit(solution)/shard_map/while
  294.9 13.2 %copy-start.2 = (bf16[24,384,1,128]{3,1,0,2:T(8,128)(2,1)S(1)}, bf16[24,384,1,128]{3,1,0,2:T(8,128)(2,1)}, u32[]{:S(2)}) copy-start(bf16[24,384,1,128]{3,1,0,2:T(8,128)(2,1)} %copy-done.1) | copy-start | bytes 7077892 | tf_op jit(solution)/shard_map/while
  308.1 1.4 copy-start.1
  319.9 8.2 %copy-start.3 = (bf16[24,384,1,128]{3,1,0,2:T(8,128)(2,1)S(1)}, bf16[24,384,1,128]{3,1,0,2:T(8,128)(2,1)}, u32[]{:S(2)}) copy-start(bf16[24,384,1,128]{3,1,0,2:T(8,128)(2,1)} %get-tuple-element.131) | copy-start | bytes 7077892 | tf_op jit(solution)/shard_map/while
  330.4 13.2 %copy-start.2 = (bf16[24,384,1,128]{3,1,0,2:T(8,128)(2,1)S(1)}, bf16[24,384,1,128]{3,1,0,2:T(8,128)(2,1)}, u32[]{:S(2)}) copy-start(bf16[24,384,1,128]{3,1,0,2:T(8,128)(2,1)} %copy-done.1) | copy-start | bytes 7077892 | tf_op jit(solution)/shard_map/while
where the time goes:
time: 398 us; the launch traced here: 393 us
  matrix products  102 us (26%)
  blocking collectives  78.4 us (20%)
  local copies, waits for them, and re-layouts  74.3 us (19%)
  other arithmetic  60.2 us (15%)
  waiting for transfers between devices  53.6 us (13%)
  starting transfers between devices  24.4 us (6%)
    dot_general x6, matrix products, attend(): jnp.einsum('ghqnt,gnthd->gqhd', weights, value_block, preferred_element_t...  59.3 us
    reduce_sum x6, other arithmetic, weigh(): summed = jnp.sum(expo, axis=(3, 4))  49.2 us
    dot_general x6, matrix products, attend(): jnp.einsum('gqhd,gnthd->ghqnt', query_block, key_block, preferred_element...  42.3 us
    all_to_all x1, blocking collectives, body(): lax.all_to_all(shaped_v, 'wide', split_axis=1, concat_axis=0, tiled=True)  39.3 us
    all_to_all x1, blocking collectives, body(): lax.all_to_all(attended, 'wide', split_axis=0, concat_axis=1, tiled=True)  39.1 us
    all_to_all x1, waiting for transfers between devices, body(): lax.all_to_all(shaped_k, 'wide', split_axis=1, concat_axis=0, tiled=True)  29.3 us
    dynamic_update_slice x12, local copies, waits for them, and re-layouts, body(): attended = lax.map(attend, (query_groups, id_groups, ok_groups))  20.1 us
    gather x6, local copies, waits for them, and re-layouts, attend(): key_block = key_tiles[id_block]  16 us
  transfers between devices with their start and end apart: 4, of which 4 were waited for; matrix products, arithmetic and copies ran while one was open for 2% of the time, Pallas kernels for 0%

commit v1 on v0

v1 whole, which is shorter than its diff:
```python
import functools
import math

import jax
import jax.numpy as jnp
from jax import lax
from jax.experimental import pallas as pl
from jax.experimental.pallas import tpu as pltpu
from jax.sharding import PartitionSpec as P

HD = 128
TILE = 384
PLANE = 6
NBR = 12
GANG = 8
UNIT = 48
PACK = 4
MESH = pl.DeviceIdType.MESH
SCALE = HD**-0.5 * math.log2(math.e)


def kernel(
    spans, wides,
    key_at, value_at, there, queries, keys, values, out,
    kbuf, vbuf, qbuf, obuf, scores,
    own_sem, ksem, vsem, qsem, send_sem, halo_sem, fwd_sem, osend_sem, orecv_sem,
):
    me = lax.axis_index("wide")
    span = lax.axis_index("span")
    above = lax.rem(span + 1, spans)
    below = lax.rem(span + spans - 1, spans)
    part = queries.shape[0]
    units = TILE // UNIT
    own_units = wides * part
    own_tiles = own_units // units
    halo = PLANE * units
    upper = halo + own_units
    half = wides // 2
    gangs = wides // GANG
    gang = me // GANG
    place = lax.rem(me, GANG)

    def columns(ref, head):
        return ref.at[:, :, pl.ds(pl.multiple_of(head * HD, HD), HD)]

    def block(ref, first, index):
        return ref.at[pl.ds(first + index * part, part)]

    def target(i):
        to = lax.rem(gang - i // GANG + gangs, gangs)
        return to * GANG + lax.rem(place + lax.rem(i, GANG), GANG)

    def source(i):
        at = lax.rem(gang + i // GANG, gangs)
        return at * GANG + lax.rem(place - lax.rem(i, GANG) + GANG, GANG)

    own = [
        pltpu.make_async_copy(columns(keys, me), block(kbuf, halo, me), own_sem.at[0]),
        pltpu.make_async_copy(columns(values, me), block(vbuf, halo, me), own_sem.at[1]),
        pltpu.make_async_copy(columns(queries, me), block(qbuf, 0, me), own_sem.at[2]),
    ]
    for copy in own:
        copy.start()

    barrier = pltpu.get_barrier_semaphore()

    def greet(i, carry):
        pl.semaphore_signal(barrier, inc=1, device_id=(span, target(i)), device_id_type=MESH)
        return carry

    lax.fori_loop(1, wides, greet, 0)
    for neighbour in (above, below):
        pl.semaphore_signal(barrier, inc=1, device_id=(neighbour, me), device_id_type=MESH)
    pl.semaphore_wait(barrier, wides + 1)

    def send(kind, i):
        ref, buf, first, sem = (
            (keys, kbuf, halo, ksem),
            (values, vbuf, halo, vsem),
            (queries, qbuf, 0, qsem),
        )[kind]
        to = target(i)
        pltpu.make_async_remote_copy(
            src_ref=columns(ref, to),
            dst_ref=block(buf, first, me),
            send_sem=send_sem.at[kind],
            recv_sem=sem.at[me],
            device_id=(span, to),
            device_id_type=MESH,
        ).start()

    def send_step(kind):
        def step(i, carry):
            send(kind, i)
            return carry
        return step

    def arrived(buf, first, sem, u):
        piece = block(buf, first, u)
        pltpu.make_async_copy(piece, piece, sem.at[u]).wait()

    def forward(kind, buf, u):
        late = u // half
        piece = block(buf, halo, u)
        place_there = block(buf, (1 - late) * upper, lax.rem(u, half))
        pltpu.make_async_remote_copy(
            src_ref=piece,
            dst_ref=place_there,
            send_sem=fwd_sem.at[kind],
            recv_sem=halo_sem.at[2 * kind + 1 - late],
            device_id=(late * above + (1 - late) * below, me),
            device_id_type=MESH,
        ).start()

    lax.fori_loop(1, wides, send_step(0), 0)
    lax.fori_loop(1, wides, send_step(1), 0)
    vbuf[pl.ds(upper + halo, units)] = jnp.zeros((units, UNIT, HD), jnp.bfloat16)

    own[0].wait()
    forward(0, kbuf, me)

    def pass_keys(i, carry):
        u = source(i)
        arrived(kbuf, halo, ksem, u)
        forward(0, kbuf, u)
        return carry

    lax.fori_loop(1, wides, pass_keys, 0)
    own[1].wait()
    forward(1, vbuf, me)

    def pass_values(i, carry):
        u = source(i)
        arrived(vbuf, halo, vsem, u)
        forward(1, vbuf, u)
        send(2, i)
        return carry

    lax.fori_loop(1, wides, pass_values, 0)
    own[2].wait()

    for kind, buf in ((0, kbuf), (1, vbuf)):
        for side, first in ((0, 0), (1, upper)):
            region = buf.at[pl.ds(first, halo)]
            pltpu.make_async_copy(region, region, halo_sem.at[2 * kind + side]).wait()

    def gang_at(step):
        return lax.rem(gang + step // 3, gangs)

    def tile_at(step):
        return gang_at(step) * 3 + lax.rem(step, 3)

    def await_queries(step):
        @pl.when(lax.rem(step, 3) == 0)
        def _():
            def one(j, carry):
                u = gang_at(step) * GANG + j

                @pl.when(u != me)
                def _():
                    arrived(qbuf, 0, qsem, u)

                return carry

            lax.fori_loop(0, GANG, one, 0)

    first_tile = span * own_tiles

    def whole(ref, first):
        return jnp.concatenate([ref[first + j] for j in range(units)], axis=0)

    def key_tile(tile, slot):
        return whole(kbuf, key_at[first_tile + tile, slot])

    def value_tile(tile, slot):
        value = whole(vbuf, value_at[first_tile + tile, slot])
        ones = jnp.full((TILE, HD), there[first_tile + tile, slot]).astype(jnp.bfloat16)
        return jnp.concatenate([value, ones], axis=1)

    def load_queries(tile):
        return qbuf[pl.ds(tile * units, units)].reshape(TILE, HD)

    def score(tile, query, pack, highest):
        key = jnp.concatenate([key_tile(tile, pack * PACK + j) for j in range(PACK)], axis=0)
        fresh = lax.dot_general(
            query, key, (((1,), (1,)), ((), ())), preferred_element_type=jnp.float32
        )
        scores[pack] = fresh
        for at in range(0, PACK * TILE, HD):
            highest = jnp.maximum(highest, fresh[:, at : at + HD])
        return highest

    def mix(tile, shift, pack, total):
        value = jnp.concatenate([value_tile(tile, pack * PACK + j) for j in range(PACK)], axis=0)
        weights = jnp.exp2(scores[pack] * SCALE - shift).astype(jnp.bfloat16)
        part = jnp.dot(weights, value, preferred_element_type=jnp.float32)
        return part if total is None else total + part

    def lowest():
        return jnp.full((TILE, HD), -jnp.inf, jnp.float32)

    def shift_of(highest):
        return jnp.max(highest, axis=1, keepdims=True) * SCALE

    def finish(step, total):
        tile = tile_at(step)
        mixed = (total[:, :HD] / total[:, HD:]).astype(jnp.bfloat16)
        obuf[pl.ds(tile * units, units)] = mixed.reshape(units, UNIT, HD)
        begin = 3 * lax.rem(step, 3) - 1

        def one(j, carry):
            @pl.when(begin + j >= 0)
            def _():
                u = gang_at(step) * GANG + begin + j

                @pl.when(u == me)
                def _():
                    pltpu.make_async_copy(
                        block(obuf, 0, u), columns(out, me), orecv_sem
                    ).start()

                @pl.when(u != me)
                def _():
                    pltpu.make_async_remote_copy(
                        src_ref=block(obuf, 0, u),
                        dst_ref=columns(out, me),
                        send_sem=osend_sem,
                        recv_sem=orecv_sem,
                        device_id=(span, u),
                        device_id_type=MESH,
                    ).start()

            return carry

        lax.fori_loop(0, 3, one, 0)

    packs = NBR // PACK
    await_queries(0)
    query = load_queries(tile_at(0))
    highest = lowest()
    for pack in range(packs):
        highest = score(tile_at(0), query, pack, highest)

    def turn(step, shift):
        await_queries(step + 1)
        tile, later = tile_at(step), tile_at(step + 1)
        query = load_queries(later)
        highest, total = lowest(), None
        for pack in range(packs):
            total = mix(tile, shift, pack, total)
            highest = score(later, query, pack, highest)
        finish(step, total)
        return shift_of(highest)

    shift = lax.fori_loop(0, own_tiles - 1, turn, shift_of(highest))
    total = None
    for pack in range(packs):
        total = mix(tile_at(own_tiles - 1), shift, pack, total)
    finish(own_tiles - 1, total)

    sent = (wides - 1) * HD
    for kind, ref in enumerate((keys, values, queries)):
        region = ref.at[:, :, pl.ds(0, sent)]
        pltpu.make_async_copy(region, region, send_sem.at[kind]).wait()
    for kind, buf in ((0, kbuf), (1, vbuf)):
        region = buf.at[pl.ds(halo, own_units)]
        pltpu.make_async_copy(region, region, fwd_sem.at[kind]).wait()
    region = obuf.at[pl.ds(0, (wides - 1) * part)]
    pltpu.make_async_copy(region, region, osend_sem).wait()
    pltpu.make_async_copy(out, out, orecv_sem).wait()


def body(spans, wides, queries, keys, values, windows):
    rows, width = queries.shape
    part = rows // UNIT
    units = TILE // UNIT
    own_units = wides * part
    near = own_units + 2 * PLANE * units
    own_tiles = own_units // units
    tiles = jnp.arange(windows.shape[0], dtype=jnp.int32)[:, None]
    first = tiles // own_tiles * own_tiles
    listed = windows >= 0
    key_at = (jnp.where(listed, windows, tiles) - first + PLANE) * units
    value_at = jnp.where(listed, key_at, near)
    cut = [a.reshape(part, UNIT, width) for a in (queries, keys, values)]
    dma = pltpu.SemaphoreType.DMA
    out = pl.pallas_call(
        functools.partial(kernel, spans, wides),
        out_shape=jax.ShapeDtypeStruct((part, UNIT, width), jnp.bfloat16),
        in_specs=[pl.BlockSpec(memory_space=pltpu.SMEM)] * 3
        + [pl.BlockSpec(memory_space=pl.ANY)] * 3,
        out_specs=pl.BlockSpec(memory_space=pl.ANY),
        scratch_shapes=[
            pltpu.VMEM((near, UNIT, HD), jnp.bfloat16),
            pltpu.VMEM((near + units, UNIT, HD), jnp.bfloat16),
            pltpu.VMEM((own_units, UNIT, HD), jnp.bfloat16),
            pltpu.VMEM((own_units, UNIT, HD), jnp.bfloat16),
            pltpu.VMEM((NBR // PACK, TILE, PACK * TILE), jnp.float32),
            dma((3,)),
            dma((wides,)),
            dma((wides,)),
            dma((wides,)),
            dma((3,)),
            dma((4,)),
            dma((2,)),
            dma(()),
            dma(()),
        ],
        compiler_params=pltpu.CompilerParams(
            collective_id=0, has_side_effects=True, vmem_limit_bytes=40 << 20
        ),
        name="attend",
    )(key_at, value_at, listed.astype(jnp.float32), *cut)
    return out.reshape(rows, width)


def solution(mesh):
    return jax.shard_map(
        functools.partial(body, mesh.shape["span"], mesh.shape["wide"]),
        mesh=mesh,
        in_specs=(
            P(("span", "wide"), None),
            P(("span", "wide"), None),
            P(("span", "wide"), None),
            P(),
        ),
        out_specs=P(("span", "wide"), None),
        check_vma=False,
    )
```

time: 398 us -> 130 us (0.33)
  the two profiles are of different devices: /device:TPU:1 before, /device:TPU:69 now
where the time goes in v1:
time: 130 us
  Pallas kernels  124 us (95%)
  local copies, waits for them, and re-layouts  5.62 us (4%)
    pallas_call x1, Pallas kernels, body(): pl.pallas_call(functools.partial(kernel, spans, wides), out_shape=jax.Sha...  124 us
    unnamed x8, local copies, waits for them, and re-layouts  5.62 us

profile of v1, /device:TPU:69, one launch (start us, length us, event | category | flops | bytes accessed | tf_op | source)
XLA Modules:
  0.0 130.2 jit_solution(7677714000514548516)
XLA Ops:
  0.0 0.8 copy.5
  0.8 0.1 broadcast_select_fusion
  0.9 0.0 copy-start
  0.9 1.3 copy-done
  2.2 0.0 copy-start.1
  2.2 1.3 copy-done.1
  3.4 0.0 copy-start.2
  3.4 1.3 copy-done.2
  4.7 124.4 %attend.1 = bf16[3,48,4096]{2,1,0:T(8,128)(2,1)S(1)} custom-call(s32[96,12]{1,0:T(8,128)S(1)} %get-tuple-element.6.key_at, s32[96,12]{1,0:T(8,128)S(1)} %get-tuple-element.5.value_at, f32[96,12]{1,0:T(8,128)S(1)} %fusion.1.there, bf16[3,48,4096]{2,1,0:T(8,128)(2,1)S(1)} %bitcast.5, bf16[3,48,4096]{2,1,0:T(8,128)(2,1)S(1)} %bitcast.6, ...), custom_call_target="tpu_custom_call" | custom-call | tf_op jit(solution)/shard_map/attend/pallas_call | solution.py:287
  129.2 1.0 copy.8
  (2 shorter events, 0.0 us)
Async XLA Ops:
  0.9 1.3 copy-start
  2.2 1.3 copy-start.1
  3.4 1.3 copy-start.2

commit v2 on v1

v2 whole, which is shorter than its diff:
```python
import functools
import math

import jax
import jax.numpy as jnp
from jax import lax
from jax.experimental import pallas as pl
from jax.experimental.pallas import tpu as pltpu
from jax.sharding import PartitionSpec as P

HD = 128
TILE = 384
PLANE = 6
NBR = 12
GANG = 8
UNIT = 48
PACK = 4
SPLITS = {2: ((0, 2, 0), (2, 1, 1)), 5: ((0, 1, 0), (1, 2, 1)), -1: ((0, 3, 0),)}
GIVES = (
    ((0, 0, 0, 3), (1, 0, 3, 3), (2, 0, 6, 2)),
    ((2, 2, 8, 1), (3, 0, 9, 3), (4, 0, 12, 3), (5, 0, 15, 1)),
    ((5, 1, 16, 2), (6, 0, 18, 3), (7, 0, 21, 3)),
)
MESH = pl.DeviceIdType.MESH
SCALE = HD**-0.5 * math.log2(math.e)


def kernel(
    spans, wides,
    windows, queries, keys, values, out,
    kbuf, vbuf, qbuf, obuf, scores,
    own_sem, ksem, vsem, qsem, send_sem, halo_sem, fwd_sem, osend_sem, orecv_sem,
):
    me = lax.axis_index("wide")
    span = lax.axis_index("span")
    above = lax.rem(span + 1, spans)
    below = lax.rem(span + spans - 1, spans)
    part = queries.shape[0]
    units = TILE // UNIT
    own_units = wides * part
    own_tiles = own_units // units
    halo = PLANE * units
    upper = halo + own_units
    half = wides // 2
    deep = half // 2
    side, depth, core = lax.div(me, half), lax.rem(lax.div(me, 2), deep), lax.rem(me, 2)

    def columns(ref, head):
        return ref.at[:, :, pl.ds(pl.multiple_of(head * HD, HD), HD)]

    def block(ref, first, index):
        return ref.at[pl.ds(first + index * part, part)]

    def peers(k, outward):
        up, down = depth + k, depth - k
        up = jnp.where(up >= deep, up - deep, up)
        down = jnp.where(down < 0, down + deep, down)
        found = []
        for j in range(4):
            there = core if j % 2 == 0 else 1 - core
            far = jnp.where(there == 1, up, down) if outward else jnp.where(core == 1, down, up)
            found.append((side if j < 2 else 1 - side, far * 2 + there))
        return found

    def every(step, outward):
        for peer in peers(0, outward)[1:]:
            step(*peer)

        def ring(k, carry):
            for peer in peers(k, outward):
                step(*peer)
            return carry

        lax.fori_loop(1, deep, ring, 0)

    own = [
        pltpu.make_async_copy(columns(keys, me), block(kbuf, halo, me), own_sem.at[0]),
        pltpu.make_async_copy(columns(values, me), block(vbuf, halo, me), own_sem.at[1]),
    ]
    for copy in own:
        copy.start()
    place_in_gang = lax.rem(me, GANG)
    own_tile = lax.div(me * part, units)
    whole_block = (place_in_gang != 2) & (place_in_gang != 5)
    for p in range(part):
        unit = me * part + p
        pltpu.make_async_copy(
            columns(queries, me).at[p], qbuf.at[unit], qsem.at[lax.div(unit, units)]
        ).start()

    barrier = pltpu.get_barrier_semaphore()

    def greet(row, place):
        to = row * half + place
        pl.semaphore_signal(barrier, inc=1, device_id=(span, to), device_id_type=MESH)

    every(greet, True)
    for neighbour in (above, below):
        pl.semaphore_signal(barrier, inc=1, device_id=(neighbour, me), device_id_type=MESH)
    pl.semaphore_wait(barrier, wides + 1)

    def send(kind, row, place):
        ref, buf, sem = ((keys, kbuf, ksem), (values, vbuf, vsem))[kind]
        to = row * half + place
        pltpu.make_async_remote_copy(
            src_ref=columns(ref, to),
            dst_ref=block(buf, halo, me),
            send_sem=send_sem.at[kind],
            recv_sem=sem.at[me],
            device_id=(span, to),
            device_id_type=MESH,
        ).start()

    def send_queries(row, place):
        to = row * half + place
        for member, pieces in SPLITS.items():
            mine = member == place_in_gang if member >= 0 else whole_block

            @pl.when(mine)
            def _():
                for begin, count, ahead in pieces:
                    pltpu.make_async_remote_copy(
                        src_ref=columns(queries, to).at[pl.ds(begin, count)],
                        dst_ref=qbuf.at[pl.ds(me * part + begin, count)],
                        send_sem=send_sem.at[2],
                        recv_sem=qsem.at[own_tile + ahead],
                        device_id=(span, to),
                        device_id_type=MESH,
                    ).start()

    def arrived(buf, sem, u):
        piece = block(buf, halo, u)
        pltpu.make_async_copy(piece, piece, sem.at[u]).wait()

    def forward(kind, buf, row, place):
        pltpu.make_async_remote_copy(
            src_ref=block(buf, halo, row * half + place),
            dst_ref=block(buf, (1 - row) * upper, place),
            send_sem=fwd_sem.at[kind],
            recv_sem=halo_sem.at[2 * kind + 1 - row],
            device_id=(row * above + (1 - row) * below, me),
            device_id_type=MESH,
        ).start()

    every(functools.partial(send, 0), True)
    every(functools.partial(send, 1), True)
    vbuf[pl.ds(upper + halo, units)] = jnp.zeros((units, UNIT, HD), jnp.bfloat16)

    def pass_on(kind, buf, sem):
        def step(row, place):
            arrived(buf, sem, row * half + place)
            forward(kind, buf, row, place)

        own[kind].wait()
        forward(kind, buf, side, depth * 2 + core)
        every(step, False)

    pass_on(0, kbuf, ksem)
    every(send_queries, True)
    pass_on(1, vbuf, vsem)

    for kind, buf in ((0, kbuf), (1, vbuf)):
        for end, first in ((0, 0), (1, upper)):
            region = buf.at[pl.ds(first, halo)]
            pltpu.make_async_copy(region, region, halo_sem.at[2 * kind + end]).wait()

    def tile_at(step):
        begin = lax.div(depth * 3 + 3, 4) - core
        turned = begin + (1 - 2 * core) * lax.div(step, 2)
        return lax.rem(side + step, 2) * PLANE + lax.rem(turned + PLANE, PLANE)

    def await_queries(step):
        tile = qbuf.at[pl.ds(tile_at(step) * units, units)]
        pltpu.make_async_copy(tile, tile, qsem.at[tile_at(step)]).wait()

    first_tile = span * own_tiles

    def whole(ref, first):
        return jnp.concatenate([ref[first + j] for j in range(units)], axis=0)

    def listed(tile, slot):
        entry = windows[slot, first_tile + tile]
        there = jnp.minimum(entry, 0) + 1
        near = jnp.clip(entry - first_tile + PLANE, 0, own_tiles + 2 * PLANE - 1)
        return there, there * near

    def key_tile(tile, slot):
        there, index = listed(tile, slot)
        return whole(kbuf, (index + (1 - there) * (tile + PLANE)) * units)

    def value_tile(tile, slot):
        there, index = listed(tile, slot)
        value = whole(vbuf, (index + (1 - there) * (own_tiles + 2 * PLANE)) * units)
        ones = jnp.full((TILE, HD), there.astype(jnp.float32)).astype(jnp.bfloat16)
        return jnp.concatenate([value, ones], axis=1)

    def load_queries(tile):
        return qbuf[pl.ds(tile * units, units)].reshape(TILE, HD)

    def score(tile, query, pack, highest):
        key = jnp.concatenate([key_tile(tile, pack * PACK + j) for j in range(PACK)], axis=0)
        fresh = lax.dot_general(
            query, key, (((1,), (1,)), ((), ())), preferred_element_type=jnp.float32
        )
        scores[pack] = fresh
        for at in range(0, PACK * TILE, HD):
            highest = jnp.maximum(highest, fresh[:, at : at + HD])
        return highest

    def mix(tile, shift, pack, total):
        value = jnp.concatenate([value_tile(tile, pack * PACK + j) for j in range(PACK)], axis=0)
        weights = jnp.exp2(scores[pack] * SCALE - shift).astype(jnp.bfloat16)
        part = jnp.dot(weights, value, preferred_element_type=jnp.float32)
        return part if total is None else total + part

    def lowest():
        return jnp.full((TILE, HD), -jnp.inf, jnp.float32)

    def shift_of(highest):
        return jnp.max(highest, axis=1, keepdims=True) * SCALE

    def finish(step, total):
        tile = tile_at(step)
        mixed = (total[:, :HD] / total[:, HD:]).astype(jnp.bfloat16)
        obuf[pl.ds(tile * units, units)] = mixed.reshape(units, UNIT, HD)

        gang = lax.div(tile, 3) * GANG
        for turn_of, pieces in enumerate(GIVES):
            @pl.when(lax.rem(tile, 3) == turn_of)
            def _():
                for place, begin, unit, count in pieces:
                    give(gang + place, begin, gang * part + unit, count)

    def give(u, begin, unit, count):
        mixed = obuf.at[pl.ds(unit, count)]
        home = columns(out, me).at[pl.ds(begin, count)]

        @pl.when(u == me)
        def _():
            pltpu.make_async_copy(mixed, home, orecv_sem).start()

        @pl.when(u != me)
        def _():
            pltpu.make_async_remote_copy(
                src_ref=mixed,
                dst_ref=home,
                send_sem=osend_sem,
                recv_sem=orecv_sem,
                device_id=(span, u),
                device_id_type=MESH,
            ).start()

    packs = NBR // PACK
    await_queries(0)
    query = load_queries(tile_at(0))
    highest = lowest()
    for pack in range(packs):
        highest = score(tile_at(0), query, pack, highest)

    def turn(step, shift):
        await_queries(step + 1)
        tile, later = tile_at(step), tile_at(step + 1)
        query = load_queries(later)
        highest, total = lowest(), None
        for pack in range(packs):
            total = mix(tile, shift, pack, total)
            highest = score(later, query, pack, highest)
        finish(step, total)
        return shift_of(highest)

    shift = lax.fori_loop(0, own_tiles - 1, turn, shift_of(highest))
    total = None
    for pack in range(packs):
        total = mix(tile_at(own_tiles - 1), shift, pack, total)
    finish(own_tiles - 1, total)

    sent = (wides - 1) * HD
    for kind, ref in enumerate((keys, values, queries)):
        region = ref.at[:, :, pl.ds(0, sent)]
        pltpu.make_async_copy(region, region, send_sem.at[kind]).wait()
    for kind, buf in ((0, kbuf), (1, vbuf)):
        region = buf.at[pl.ds(halo, own_units)]
        pltpu.make_async_copy(region, region, fwd_sem.at[kind]).wait()
    region = obuf.at[pl.ds(0, (wides - 1) * part)]
    pltpu.make_async_copy(region, region, osend_sem).wait()
    pltpu.make_async_copy(out, out, orecv_sem).wait()


def body(spans, wides, queries, keys, values, windows):
    rows, width = queries.shape
    part = rows // UNIT
    units = TILE // UNIT
    own_units = wides * part
    near = own_units + 2 * PLANE * units
    cut = [a.reshape(part, UNIT, width) for a in (queries, keys, values)]
    dma = pltpu.SemaphoreType.DMA
    out = pl.pallas_call(
        functools.partial(kernel, spans, wides),
        out_shape=jax.ShapeDtypeStruct((part, UNIT, width), jnp.bfloat16),
        in_specs=[pl.BlockSpec(memory_space=pltpu.SMEM)]
        + [pl.BlockSpec(memory_space=pltpu.HBM)] * 3,
        out_specs=pl.BlockSpec(memory_space=pl.ANY),
        scratch_shapes=[
            pltpu.VMEM((near, UNIT, HD), jnp.bfloat16),
            pltpu.VMEM((near + units, UNIT, HD), jnp.bfloat16),
            pltpu.VMEM((own_units, UNIT, HD), jnp.bfloat16),
            pltpu.VMEM((own_units, UNIT, HD), jnp.bfloat16),
            pltpu.VMEM((NBR // PACK, TILE, PACK * TILE), jnp.float32),
            dma((2,)),
            dma((wides,)),
            dma((wides,)),
            dma((own_units // units,)),
            dma((3,)),
            dma((4,)),
            dma((2,)),
            dma(()),
            dma(()),
        ],
        compiler_params=pltpu.CompilerParams(
            collective_id=0, has_side_effects=True, vmem_limit_bytes=60 << 20
        ),
        name="attend",
    )(windows.T, *cut)
    return out.reshape(rows, width)


def solution(mesh):
    return jax.shard_map(
        functools.partial(body, mesh.shape["span"], mesh.shape["wide"]),
        mesh=mesh,
        in_specs=(
            P(("span", "wide"), None),
            P(("span", "wide"), None),
            P(("span", "wide"), None),
            P(),
        ),
        out_specs=P(("span", "wide"), None),
        check_vma=False,
    )
```

time: 130 us -> 119 us (0.915)
  the two profiles are of different devices: /device:TPU:69 before, /device:TPU:1 now
where the time goes in v2:
time: 119 us
  Pallas kernels  116 us (97%)
  local copies, waits for them, and re-layouts  2.39 us (2%)
    pallas_call x1, Pallas kernels, body(): pl.pallas_call(functools.partial(kernel, spans, wides), out_shape=jax.Sha...  116 us
    unnamed x1, local copies, waits for them, and re-layouts  2.39 us

profile of v2, /device:TPU:1, one launch (start us, length us, event | category | flops | bytes accessed | tf_op | source)
XLA Modules:
  0.0 118.9 jit_solution(5672589318926832439)
XLA Ops:
  0.0 116.5 %attend.1 = bf16[3,48,4096]{2,1,0:T(8,128)(2,1)} custom-call(s32[12,96]{1,0:T(8,128)} %bitcast.9, bf16[3,48,4096]{2,1,0:T(8,128)(2,1)} %bitcast.6, bf16[3,48,4096]{2,1,0:T(8,128)(2,1)} %bitcast.7, bf16[3,48,4096]{2,1,0:T(8,128)(2,1)} %bitcast.8), custom_call_target="tpu_custom_call" | custom-call | tf_op jit(solution)/shard_map/attend/pallas_call | solution.py:297
  116.5 2.4 %copy.6 = bf16[144,4096]{1,0:T(8,128)(2,1)} copy(bf16[144,4096]{1,0:T(8,128)(2,1)} %bitcast.5) | data formatting | bytes 2359296

commit v3 on v2

--- a/solution.py
+++ b/solution.py
@@ -293,6 +293,9 @@
     own_units = wides * part
     near = own_units + 2 * PLANE * units
     cut = [a.reshape(part, UNIT, width) for a in (queries, keys, values)]
+    windows, *cut = [
+        pltpu.with_memory_space_constraint(a, pltpu.HBM) for a in (windows.T, *cut)
+    ]
     dma = pltpu.SemaphoreType.DMA
     out = pl.pallas_call(
         functools.partial(kernel, spans, wides),
@@ -317,10 +320,10 @@
             dma(()),
         ],
         compiler_params=pltpu.CompilerParams(
-            collective_id=0, has_side_effects=True, vmem_limit_bytes=60 << 20
+            collective_id=0, has_side_effects=True, vmem_limit_bytes=48 << 20
         ),
         name="attend",
-    )(windows.T, *cut)
+    )(windows, *cut)
     return out.reshape(rows, width)
 
 

time: 119 us -> 118 us (level)
  local copies, waits for them, and re-layouts: 2.39 us -> 1.02 us
    unnamed x1, local copies, waits for them, and re-layouts: 2.39 us -> 1.02 us
where the time goes in v3:
time: 118 us; the launch traced here: 117 us
  Pallas kernels  116 us (98%)
    pallas_call x1, Pallas kernels, body(): pl.pallas_call(functools.partial(kernel, spans, wides), out_shape=jax.Sha...  116 us

profile of v3, /device:TPU:1, one launch (start us, length us, event | category | flops | bytes accessed | tf_op | source)
XLA Modules:
  0.0 117.4 jit_solution(1458685365591444310)
XLA Ops:
  0.0 116.4 %attend.1 = bf16[3,48,4096]{2,1,0:T(8,128)(2,1)S(1)} custom-call(s32[12,96]{1,0:T(8,128)} %bitcast.9, bf16[3,48,4096]{2,1,0:T(8,128)(2,1)} %bitcast.6, bf16[3,48,4096]{2,1,0:T(8,128)(2,1)} %bitcast.7, bf16[3,48,4096]{2,1,0:T(8,128)(2,1)} %bitcast.8), custom_call_target="tpu_custom_call" | custom-call | tf_op jit(solution)/shard_map/attend/pallas_call | solution.py:300
  116.4 1.0 copy.6

commit v4 on v3

--- a/solution.py
+++ b/solution.py
@@ -62,6 +62,17 @@
             found.append((side if j < 2 else 1 - side, far * 2 + there))
         return found
 
+    def far_first(step, outward):
+        def ring(m, carry):
+            k = deep // 2 + lax.div(m + 1, 2) * (1 - 2 * lax.rem(m, 2))
+            for peer in peers(k, outward):
+                step(*peer)
+            return carry
+
+        lax.fori_loop(0, deep - 1, ring, 0)
+        for peer in peers(0, outward)[1:]:
+            step(*peer)
+
     def every(step, outward):
         for peer in peers(0, outward)[1:]:
             step(*peer)
@@ -94,9 +105,9 @@
         to = row * half + place
         pl.semaphore_signal(barrier, inc=1, device_id=(span, to), device_id_type=MESH)
 
-    every(greet, True)
     for neighbour in (above, below):
         pl.semaphore_signal(barrier, inc=1, device_id=(neighbour, me), device_id_type=MESH)
+    far_first(greet, True)
     pl.semaphore_wait(barrier, wides + 1)
 
     def send(kind, row, place):

time: 118 us -> 117 us (level)
  no operation moved by 1% of the time
where the time goes in v4:
time: 117 us
  Pallas kernels  116 us (99%)
    pallas_call x1, Pallas kernels, body(): pl.pallas_call(functools.partial(kernel, spans, wides), out_shape=jax.Sha...  116 us

profile of v4, /device:TPU:1, one launch (start us, length us, event | category | flops | bytes accessed | tf_op | source)
XLA Modules:
  0.0 117.2 jit_solution(2244885568384314439)
XLA Ops:
  0.0 116.2 %attend.1 = bf16[3,48,4096]{2,1,0:T(8,128)(2,1)S(1)} custom-call(s32[12,96]{1,0:T(8,128)} %bitcast.9, bf16[3,48,4096]{2,1,0:T(8,128)(2,1)} %bitcast.6, bf16[3,48,4096]{2,1,0:T(8,128)(2,1)} %bitcast.7, bf16[3,48,4096]{2,1,0:T(8,128)(2,1)} %bitcast.8), custom_call_target="tpu_custom_call" | custom-call | tf_op jit(solution)/shard_map/attend/pallas_call | solution.py:311
  116.2 1.0 copy.6
